TPU v7x, 256 devices: a whole 4x4x8 slice. The times are simulated.
256 devices in a mesh: ka: 8 (over z_lo, x), ta: 32 (over y, z_hi, core).
Axes of the slice: x: 4, y: 4, z: 8 (z_hi: 4, z_lo: 2; z = z_hi * 2 + z_lo), core: 2. Of those that a mesh axis runs over, the one named last changes fastest.
Arguments:
- amplitudes: float32 [6144, 6144], P('ta', 'ka'), may hold values from -6 to 6
- driving: float32 [6144, 6144], P('ta', 'ka'), may hold values from -24 to 24
- cycle_ints: bfloat16 [6144, 6144], P('ka', 'ta'), may hold values from -0.078125 to 0.078125
- occ_irrep: int32 [128], replicated, may hold values from 0 to 3
- vir_irrep: int32 [1536], replicated, may hold values from 0 to 3
- occ_energy: float32 [128], replicated, may hold values from -2 to -0.5
- vir_energy: float32 [1536], replicated, may hold values from 0.3 to 3
- slab: int32 [4], replicated, may hold values from 0 to 127
Outputs:
- updated: float32 [6144, 6144], P('ta', 'ka')
Inputs may be any that keep to these rules, and one draw needn't show every extreme that they name: `slab`: slab positions may name the same occupied orbital more than once.
All inputs are finite; a program needn't handle non-finite values.
Results may differ from a plain program's by a relative error of at most 0.00048.
Values may be sent and summed in bfloat16 or wider, within the bound.
A program may use at most 64 MiB of HBM per device.

v0:
```python
import jax
import jax.numpy as jnp
from jax import lax
from jax.sharding import PartitionSpec as P

ITERS = 2


def labels(occ_irrep, vir_irrep, occ_energy, vir_energy, slab):
    picked = slab[:, None] == jnp.arange(occ_irrep.shape[0], dtype=jnp.int32)[None, :]
    slab_irrep = jnp.sum(jnp.where(picked, occ_irrep[None, :], 0), axis=1)
    slab_energy = jnp.sum(jnp.where(picked, occ_energy[None, :], 0.0), axis=1)
    irrep = jnp.bitwise_xor(slab_irrep[:, None], vir_irrep[None, :]).reshape(-1)
    energy = (vir_energy[None, :] - slab_energy[:, None]).reshape(-1)
    return (irrep, energy)


def local(amplitudes, driving, cycle_ints, occ_irrep, vir_irrep, occ_energy, vir_energy, slab):
    n_ka = lax.axis_size("ka")
    n_ta = lax.axis_size("ta")
    tile_rows, tile_cols = amplitudes.shape
    block = tile_rows // n_ka
    row_owner = lax.axis_index("ta")
    col_owner = lax.axis_index("ka")
    irrep, energy = labels(occ_irrep, vir_irrep, occ_energy, vir_energy, slab)
    row_irrep = lax.dynamic_index_in_dim(
        irrep.reshape(n_ta, tile_rows), row_owner, 0, keepdims=False
    )
    row_energy = lax.dynamic_index_in_dim(
        energy.reshape(n_ta, tile_rows), row_owner, 0, keepdims=False
    )
    col_irrep = lax.dynamic_index_in_dim(
        irrep.reshape(n_ta, n_ka, block), col_owner, 1, keepdims=False
    ).reshape(-1)
    col_energy = lax.dynamic_index_in_dim(
        energy.reshape(n_ta, n_ka, block), col_owner, 1, keepdims=False
    ).reshape(-1)
    mask = row_irrep[:, None] == col_irrep[None, :]
    denom = row_energy[:, None] + col_energy[None, :]
    k_rows = cycle_ints.shape[0]
    gathered = lax.all_gather(cycle_ints, "ta", axis=1, tiled=True)
    whole = (
        gathered.reshape(k_rows, n_ta, n_ka, block)
        .transpose(0, 2, 1, 3)
        .reshape(k_rows, n_ta * n_ka * block)
    )
    current = amplitudes
    for step in range(ITERS):
        operand = current.astype(jnp.bfloat16)
        partial_value = jnp.dot(operand, whole, preferred_element_type=jnp.float32)
        own_cycle = lax.psum_scatter(partial_value, "ka", scatter_dimension=1, tiled=True)
        received = lax.all_to_all(
            lax.all_to_all(own_cycle, "ta", split_axis=1, concat_axis=1, tiled=True),
            "ka",
            split_axis=0,
            concat_axis=0,
            tiled=True,
        )
        mirrored = (
            received.reshape(n_ka, block, n_ta, block)
            .transpose(0, 3, 2, 1)
            .reshape(tile_rows, tile_cols)
        )
        total = driving + own_cycle + mirrored
        current = jnp.where(mask, -total / denom, 0.0)
    return current


def solution(mesh):
    in_specs = (P("ta", "ka"), P("ta", "ka"), P("ka", "ta"), P(), P(), P(), P(), P())
    out_specs = P("ta", "ka")
    return jax.shard_map(local, mesh=mesh, in_specs=in_specs, out_specs=out_specs, check_vma=False)
```

profile of v0, /device:TPU:1, one launch (start us, length us, event | category | flops | bytes accessed | tf_op | source)
XLA Modules:
  0.0 374.1 jit_solution(14976489246637795100)
XLA Ops:
  6.5 0.7 all-gather.2.cloned.1.call-update
  7.3 90.9 %all-gather.2.cloned.1.call-done = bf16[768,6144]{0,1:T(8,128)(2,1)} async-done(((bf16[768,192]{0,1:T(8,128)(2,1)}), bf16[768,6144]{0,1:T(8,128)(2,1)}) %all-gather.2.cloned.1.call-update) | async-done | bytes 9437200 | tf_op jit(solution)/shard_map/all_gather | solution.py:41
  98.2 8.0 %copy.25 = bf16[768,8,32,24]{0,3,2,1:T(8,128)(2,1)} copy(bf16[768,8,32,24]{0,3,1,2:T(8,128)(2,1)} %bitcast.36) | data formatting | bytes 18874368 | tf_op jit(solution)/shard_map/transpose | solution.py:44
  106.2 9.1 %fusion.6 = f32[192,6144]{1,0:T(8,128)} fusion(bf16[768,6144]{0,1:T(8,128)(2,1)} %bitcast.32, f32[192,768]{1,0:T(8,128)S(1)} %copy-done), kind=kOutput, calls=%fused_computation.9 | convolution fusion | flops 1812086784 | bytes 14745600 | tf_op jit(solution)/shard_map/dot_general | solution.py:50
  115.4 58.6 %reduce-scatter.3.cloned.1.call-done = f32[192,768]{1,0:T(8,128)} async-done(((f32[192,6144]{1,0:T(8,128)}), f32[192,768]{1,0:T(8,128)}) %reduce-scatter.3.cloned.1.call-update) | async-done | bytes 589840 | tf_op jit(solution)/shard_map/reduce_scatter | solution.py:51
  174.0 2.2 copy.26
  176.2 9.4 %all-to-all-start = ((f32[192,32,24]{0,2,1:T(8,128)}), f32[192,32,24]{0,2,1:T(8,128)}, u32[]{:S(2)}, u32[]{:S(2)}) async-start(f32[192,32,24]{0,2,1:T(8,128)} %bitcast.6), calls=%async_computation.1 | async-start | bytes 1572864 | tf_op jit(solution)/shard_map/all_to_all | solution.py:53
  186.0 0.2 select_reduce_fusion
  186.5 0.6 dynamic-slice.1
  187.4 0.7 dynamic-slice
  188.1 19.0 %all-to-all-done = f32[192,32,24]{0,2,1:T(8,128)} async-done(((f32[192,32,24]{0,2,1:T(8,128)}), f32[192,32,24]{0,2,1:T(8,128)}, u32[]{:S(2)}, u32[]{:S(2)}) %all-to-all-start) | async-done | bytes 589856 | tf_op jit(solution)/shard_map/all_to_all | solution.py:53
  207.1 2.1 reshape.65
  209.2 1.8 copy.33
  211.0 5.4 %all-to-all-start.1 = ((f32[8,24,768]{2,1,0:T(8,128)}), f32[8,24,768]{2,1,0:T(8,128)}, u32[]{:S(2)}, u32[]{:S(2)}) async-start(f32[8,24,768]{2,1,0:T(8,128)} %copy.33), calls=%async_computation.2 | async-start | bytes 1179648 | tf_op jit(solution)/shard_map/all_to_all | solution.py:52
  216.5 0.2 reduce-scatter.5.cloned.1.call-start
  216.9 0.6 dynamic-slice_subtract_fusion.1
  217.5 0.7 dynamic-slice_xor_fusion.1
  218.2 8.4 %all-to-all-done.1 = f32[8,24,768]{2,1,0:T(8,128)} async-done(((f32[8,24,768]{2,1,0:T(8,128)}), f32[8,24,768]{2,1,0:T(8,128)}, u32[]{:S(2)}, u32[]{:S(2)}) %all-to-all-start.1) | async-done | bytes 589856 | tf_op jit(solution)/shard_map/all_to_all | solution.py:52
  226.6 3.3 reshape.61
  229.9 4.0 %copy.28 = f32[8,24,32,24]{3,2,1,0:T(8,128)} copy(f32[8,24,32,24]{1,2,3,0:T(8,128)S(1)} %bitcast.34) | data formatting | bytes 1179648 | tf_op jit(solution)/shard_map/transpose | solution.py:61
  233.9 3.2 reshape.62
  237.2 9.5 %fusion.1 = f32[192,6144]{1,0:T(8,128)} fusion(bf16[768,6144]{0,1:T(8,128)(2,1)} %bitcast.33, f32[192,768]{1,0:T(8,128)S(1)} %reshape.62, f32[192,768]{1,0:T(8,128)} %param.9, f32[192,768]{1,0:T(8,128)} %reduce-scatter.3.cloned.1.call-done, f32[768]{0:T(1024)S(1)} %add.51, f32[192]{0:T(256)S(1)} %bitcast.38, s32[768]{0:T(1024)S(1)} %eq.35, s32[192]{0:T(256)S(1)} %bitcast.40), kind=kOutput, calls=%fused_computation.5 | convolution fusion | flops 1813118976 | bytes 15932928 | tf_op jit(solution)/shard_map/dot_general | solution.py:50
  246.8 56.2 %reduce-scatter.5.cloned.1.call-done = f32[192,768]{1,0:T(8,128)} async-done(((f32[192,6144]{1,0:T(8,128)}), f32[192,768]{1,0:T(8,128)}) %reduce-scatter.5.cloned.1.call-update) | async-done | bytes 589840 | tf_op jit(solution)/shard_map/reduce_scatter | solution.py:51
  303.0 1.3 copy.30
  304.3 30.8 %all_to_all.36 = f32[192,32,24]{0,2,1:T(8,128)} all-to-all(f32[192,32,24]{0,2,1:T(8,128)S(1)} %bitcast.37), channel_id=1, replica_groups=mesh['ka'=8,'ta'=32] {'ta'}, dimensions={1} | all-to-all | bytes 1179648 | tf_op jit(solution)/shard_map/all_to_all | solution.py:53
  335.1 2.1 reshape.66
  337.1 1.8 copy.34
  339.0 15.7 %all_to_all.37 = f32[8,24,768]{2,1,0:T(8,128)} all-to-all(f32[8,24,768]{2,1,0:T(8,128)} %copy.34), channel_id=1, replica_groups=mesh['ka'=8,'ta'=32] {'ka'}, dimensions={0} | all-to-all | bytes 1179648 | tf_op jit(solution)/shard_map/all_to_all | solution.py:52
  354.7 3.3 reshape.63
  358.0 4.0 %copy.32 = f32[8,24,32,24]{3,2,1,0:T(8,128)} copy(f32[8,24,32,24]{1,2,3,0:T(8,128)S(1)} %bitcast.35) | data formatting | bytes 1179648 | tf_op jit(solution)/shard_map/transpose | solution.py:61
  362.0 3.2 reshape.64
  365.3 2.3 compare_select_fusion
  (35 shorter events, 1.3 us)
Async XLA Ops:
  6.5 91.7 %all-gather.2.cloned.1.call-start = ((), (), s32[]{:S(2)}) async-start(), calls=%async_computation.6 | async-start | bytes 9732096 | tf_op jit(solution)/shard_map/all_gather | solution.py:41
  7.3 166.7 %reduce-scatter.3.cloned.1.call-start = ((), (), s32[]{:S(2)}) async-start(), calls=%async_computation.7 | async-start | bytes 5308416 | tf_op jit(solution)/shard_map/reduce_scatter | solution.py:51
  98.2 8.0 %copy-start = (f32[192,768]{1,0:T(8,128)S(1)}, f32[192,768]{1,0:T(8,128)}, u32[]{:S(2)}) copy-start(f32[192,768]{1,0:T(8,128)} %param.8) | copy-start | bytes 1769476
  115.3 70.3 %copy-start.1 = (f32[1536]{0:T(1024)S(1)}, f32[1536]{0:T(1024)}, u32[]{:S(2)}) copy-start(f32[1536]{0:T(1024)} %param.14) | copy-start | bytes 18436
  115.3 70.5 %copy-start.2 = (s32[1536]{0:T(1024)S(1)}, s32[1536]{0:T(1024)}, u32[]{:S(2)}) copy-start(s32[1536]{0:T(1024)} %param.12) | copy-start | bytes 18436
  115.3 70.6 %copy-start.3 = (f32[128]{0:T(128)S(1)}, f32[128]{0:T(128)}, u32[]{:S(2)}) copy-start(f32[128]{0:T(128)} %param.13) | copy-start | bytes 1540
  115.3 70.6 %copy-start.4 = (s32[4]{0:T(128)S(1)}, s32[4]{0:T(128)}, u32[]{:S(2)}) copy-start(s32[4]{0:T(128)} %param.15) | copy-start | bytes 52
  115.3 71.8 %copy-start.5 = (s32[128]{0:T(128)S(1)}, s32[128]{0:T(128)}, u32[]{:S(2)}) copy-start(s32[128]{0:T(128)} %param.11) | copy-start | bytes 1540
  176.2 30.9 %all-to-all-start = ((f32[192,32,24]{0,2,1:T(8,128)}), f32[192,32,24]{0,2,1:T(8,128)}, u32[]{:S(2)}, u32[]{:S(2)}) async-start(f32[192,32,24]{0,2,1:T(8,128)} %bitcast.6), calls=%async_computation.1 | async-start | bytes 1572864 | tf_op jit(solution)/shard_map/all_to_all | solution.py:53
  211.0 15.6 %all-to-all-start.1 = ((f32[8,24,768]{2,1,0:T(8,128)}), f32[8,24,768]{2,1,0:T(8,128)}, u32[]{:S(2)}, u32[]{:S(2)}) async-start(f32[8,24,768]{2,1,0:T(8,128)} %copy.33), calls=%async_computation.2 | async-start | bytes 1179648 | tf_op jit(solution)/shard_map/all_to_all | solution.py:52
  216.5 86.5 %reduce-scatter.5.cloned.1.call-start = ((), (), s32[]{:S(2)}) async-start(), calls=%async_computation.8 | async-start | bytes 5308416 | tf_op jit(solution)/shard_map/reduce_scatter | solution.py:51
Sparse Core Ops, SparseCore 0:
  9.9 88.2 all-gather.1
  115.5 58.4 reduce-scatter.2
  246.9 56.0 reduce-scatter.4
where the time goes:
time: 375 us; the launch traced here: 374 us
  waiting for transfers between devices  234 us (62%)
  blocking collectives  46.5 us (12%)
  local copies, waits for them, and re-layouts  42.6 us (11%)
  matrix products  18.7 us (5%)
  starting transfers between devices  15.1 us (4%)
  between operations  13.3 us (4%)
  other arithmetic  4.1 us (1%)
    reduce_scatter x2, waiting for transfers between devices, local(): lax.psum_scatter(partial_value, 'ka', scatter_dimension=1, tiled=True)  115 us
    all_gather x1, waiting for transfers between devices, local(): gathered = lax.all_gather(cycle_ints, 'ta', axis=1, tiled=True)  90.9 us
    all_to_all x1, blocking collectives, local(): lax.all_to_all(own_cycle, 'ta', split_axis=1, concat_axis=1, tiled=True)  30.8 us
    all_to_all x1, waiting for transfers between devices, local(): lax.all_to_all(own_cycle, 'ta', split_axis=1, concat_axis=1, tiled=True)  19 us
    dot_general x2, matrix products, local(): partial_value = jnp.dot(operand, whole, preferred_element_type=jnp.float32)  18.7 us
    all_to_all x1, blocking collectives, local(): lax.all_to_all(lax.all_to_all(own_cycle, 'ta', split_axis=1, concat_axis=...  15.7 us
    all_to_all x1, starting transfers between devices, local(): lax.all_to_all(own_cycle, 'ta', split_axis=1, concat_axis=1, tiled=True)  9.38 us
    all_to_all x1, waiting for transfers between devices, local(): lax.all_to_all(lax.all_to_all(own_cycle, 'ta', split_axis=1, concat_axis=...  8.41 us
  transfers between devices with their start and end apart: 5, of which 5 were waited for; matrix products, arithmetic and copies ran while one was open for 1% of the time, Pallas kernels for 0%

commit v1 on v0

v1 whole, which is shorter than its diff:
```python
import functools

import jax
import jax.numpy as jnp
from jax import lax
from jax.experimental import pallas as pl
from jax.experimental.pallas import tpu as pltpu
from jax.sharding import PartitionSpec as P

ITERS = 2
MESH = pl.DeviceIdType.MESH
NT = (((1,), (1,)), ((), ()))


def labels(occ_irrep, vir_irrep, occ_energy, vir_energy, slab):
    picked = slab[:, None] == jnp.arange(occ_irrep.shape[0], dtype=jnp.int32)[None, :]
    slab_irrep = jnp.sum(jnp.where(picked, occ_irrep[None, :], 0), axis=1)
    slab_energy = jnp.sum(jnp.where(picked, occ_energy[None, :], 0.0), axis=1)
    irrep = jnp.bitwise_xor(slab_irrep[:, None], vir_irrep[None, :]).reshape(-1)
    energy = (vir_energy[None, :] - slab_energy[:, None]).reshape(-1)
    return (irrep, energy)


def kernel(amp, drv, rloc, rowe, cole, rowi, coli, out,
           rpair, rsend, rt, ball, ct, u, xs, m,
           p_s, p_r, a_s, a_r, b_s, b_r, z_s, y_s, c_s, r_r, c_r, u_s, u_r, m_s, m_r):
    s = lax.axis_index("ka")
    t = lax.axis_index("ta")
    zlo, x = s // 4, s % 4
    y, zhi, core = t // 8, (t // 2) % 4, t % 2
    j = t // 2
    other = 1 - core

    def dev_t(yy, zz, cc):
        return (s, (yy * 4 + zz) * 2 + cc)

    zpart = ((1 - zlo) * 4 + x, t)
    cpart = dev_t(y, zhi, other)
    kpeers = [(s + d) % 8 for d in range(1, 8)]
    greet = [(q, t) for q in kpeers] + [cpart]
    greet += [dev_t(y, (zhi + d) % 4, core) for d in (1, 2, 3)]
    greet += [dev_t((y + d) % 4, zhi, core) for d in (1, 2, 3)]
    barrier = pltpu.get_barrier_semaphore()
    for peer in greet:
        pl.semaphore_signal(barrier, inc=1, device_id=peer, device_id_type=MESH)
    pl.semaphore_wait(barrier, len(greet))

    pending = []

    def send(src, dst, ss, rs, peer):
        copy = pltpu.make_async_remote_copy(
            src_ref=src, dst_ref=dst, send_sem=ss, recv_sem=rs, device_id=peer, device_id_type=MESH)
        copy.start()
        pending.append(copy)

    def arrived(dst, rs):
        pltpu.make_async_remote_copy(
            src_ref=dst, dst_ref=dst, send_sem=p_s, recv_sem=rs, device_id=cpart, device_id_type=MESH).wait_recv()

    send(rloc, rpair, p_s, p_r, cpart)

    def spread_b(it):
        mine = ball.at[it, s]
        send(mine, mine, b_s.at[it, 0], b_r.at[it, s], zpart)
        for d in (1, 3, 2):
            send(mine, mine, b_s.at[it, d], b_r.at[it, s], (zlo * 4 + (x + d) % 4, t))

    def relay_b(it):
        q = (1 - zlo) * 4 + x
        arrived(ball.at[it, q], b_r.at[it, q])
        for d in (1, 3, 2):
            send(ball.at[it, q], ball.at[it, q], b_s.at[it, 3 + d], b_r.at[it, q], (zlo * 4 + (x + d) % 4, t))

    def await_b(it):
        for z in (0, 1):
            for d in (1, 3, 2):
                q = (zlo + z) % 2 * 4 + (x + d) % 4
                arrived(ball.at[it, q], b_r.at[it, q])

    ball[0, s] = amp[...].astype(jnp.bfloat16)
    spread_b(0)

    arrived(rpair, p_r)
    own_first = core == 0
    for q in range(8):
        a = rloc[q].astype(jnp.float32)
        b = rpair[q].astype(jnp.float32)
        both = jnp.concatenate([jnp.where(own_first, a, b), jnp.where(own_first, b, a)], axis=0).astype(jnp.bfloat16)
        rsend[q] = jnp.where(own_first, both[:, :384], both[:, 384:])
    base = pl.multiple_of(core * 3072, 3072)

    def kslot(q):
        return pl.ds(pl.multiple_of(base + q * 384, 384), 384)

    rt[j, :, kslot(s)] = rsend[s]
    for d in range(1, 8):
        q = (s + d) % 8
        send(rsend.at[q], rt.at[j, :, kslot(s)], a_s.at[d], a_r.at[s], (q, t))
    for d in range(1, 8):
        q = (s + d) % 8
        arrived(rt.at[j, :, kslot(q)], a_r.at[q])

    def piece(jj, p, c=None):
        start = (core if c is None else c) * 3072 + p * 1536
        return rt.at[jj, :, pl.ds(pl.multiple_of(start, 1536), 1536)]

    def to_y(i, jj):
        for p in (0, 1):
            send(piece(jj, p), piece(jj, p), y_s.at[i, 0, p], r_r.at[jj, p], dev_t((y + 1) % 4, zhi, core))
            send(piece(jj, p), piece(jj, p), y_s.at[i, 1, p], r_r.at[jj, p], dev_t((y + 3) % 4, zhi, core))

    def to_core(i, jj, p):
        send(piece(jj, p), piece(jj, p), c_s.at[i, p], c_r.at[jj, p], cpart)

    for p in (0, 1):
        to_core(0, j, p)
    to_y(0, j)
    for p in (0, 1):
        for d in (1, 3, 2):
            send(piece(j, p), piece(j, p), z_s.at[d, p], r_r.at[j, p], dev_t(y, (zhi + d) % 4, core))
    relay_b(0)
    for i, d in ((1, 1), (2, 3), (3, 2)):
        jj = y * 4 + (zhi + d) % 4
        for p in (0, 1):
            arrived(piece(jj, p), r_r.at[jj, p])
            to_core(i, jj, p)
        to_y(i, jj)

    def group(it, yy):
        def step(k, acc):
            h, q = k // 8, k % 8
            left = rt[pl.ds(yy * 4, 4), :, pl.ds(pl.multiple_of(k * 384, 384), 384)].reshape(192, 384)
            right = ball[it, q, :, pl.ds(pl.multiple_of(h * 384, 384), 384)]
            return acc + lax.dot_general(left, right, NT, preferred_element_type=jnp.float32)
        acc = lax.fori_loop(0, 16, step, jnp.zeros((192, 192), jnp.float32))
        ct[it, pl.ds(yy * 8, 8)] = acc.reshape(8, 24, 192)

    def mirror_a(it, g, yy):
        for e in range(8):
            tt = yy * 8 + (t + e) % 8
            k = g * 8 + e
            if k == 0:
                u[it, t] = ct[it, t]
            else:
                send(ct.at[it, tt], u.at[it, t], u_s.at[it, k], u_r.at[it, t], (s, tt))

    def mirror_b(it):
        for g in range(4):
            for e in range(8):
                if g + e:
                    tt = (y + g) % 4 * 8 + (t + e) % 8
                    arrived(u.at[it, tt], u_r.at[it, tt])
        for q in range(8):
            xs[it, q] = jnp.concatenate([u[it, i, :, q * 24:(q + 1) * 24] for i in range(32)], axis=1)
        m[it, s] = xs[it, s]
        for d in range(1, 8):
            q = (s + d) % 8
            send(xs.at[it, q], m.at[it, s], m_s.at[it, d], m_r.at[it, s], (q, t))

    def total(it):
        c = jnp.concatenate([ct[it].reshape(768, 192), jnp.zeros((768, 64), jnp.float32)], axis=1).T[:192]
        for d in range(1, 8):
            q = (s + d) % 8
            arrived(m.at[it, q], m_r.at[it, q])
        return drv[...] + c + m[it].reshape(192, 768)

    await_b(0)
    for g, d in enumerate((0, 1, 3, 2)):
        yy = (y + d) % 4
        for i, e in enumerate((0, 1, 3, 2)):
            jj = yy * 4 + (zhi + e) % 4
            for p in (0, 1):
                if g:
                    arrived(piece(jj, p), r_r.at[jj, p])
                    to_core(g * 4 + i, jj, p)
                if (g, p) == (1, 1):
                    send(piece(jj, p), piece(jj, p), y_s.at[i, 2, p], r_r.at[jj, p], dev_t((y + 3) % 4, zhi, core))
                if (g, p) == (2, 0):
                    send(piece(jj, p), piece(jj, p), y_s.at[i, 2, p], r_r.at[jj, p], dev_t((y + 1) % 4, zhi, core))
        for i, e in enumerate((0, 1, 3, 2)):
            jj = yy * 4 + (zhi + e) % 4
            for p in (0, 1):
                arrived(piece(jj, p, other), c_r.at[jj, p])
        group(0, yy)
        mirror_a(0, g, yy)
    mirror_b(0)
    tot = total(0)
    keep = rowi[...] == coli[...]
    nxt = jnp.where(keep, -tot / (rowe[...] + cole[...]), 0.0)
    ball[1, s] = nxt.astype(jnp.bfloat16)
    spread_b(1)
    relay_b(1)
    await_b(1)
    for g, d in enumerate((0, 1, 3, 2)):
        yy = (y + d) % 4
        group(1, yy)
        mirror_a(1, g, yy)
    mirror_b(1)
    out[...] = total(1)
    for copy in pending:
        copy.wait_send()


def local(amplitudes, driving, cycle_ints, occ_irrep, vir_irrep, occ_energy, vir_energy, slab):
    n_ka = lax.axis_size("ka")
    n_ta = lax.axis_size("ta")
    rows, cols = amplitudes.shape
    block = rows // n_ka
    t, s = lax.axis_index("ta"), lax.axis_index("ka")
    irrep, energy = labels(occ_irrep, vir_irrep, occ_energy, vir_energy, slab)
    pick = functools.partial(lax.dynamic_index_in_dim, keepdims=False)
    rowi = pick(irrep.reshape(n_ta, rows), t, 0).reshape(rows, 1)
    rowe = pick(energy.reshape(n_ta, rows), t, 0).reshape(rows, 1)
    coli = pick(irrep.reshape(n_ta, n_ka, block), s, 1).reshape(1, cols)
    cole = pick(energy.reshape(n_ta, n_ka, block), s, 1).reshape(1, cols)
    rloc = cycle_ints.T.reshape(n_ka, block, cols)
    f32, bf16 = jnp.float32, jnp.bfloat16
    dma = pltpu.SemaphoreType.DMA
    tot = pl.pallas_call(
        kernel,
        out_shape=jax.ShapeDtypeStruct((rows, cols), f32),
        in_specs=[pl.BlockSpec(memory_space=pltpu.VMEM)] * 7,
        out_specs=pl.BlockSpec(memory_space=pltpu.VMEM),
        scratch_shapes=[
            pltpu.VMEM((8, 24, 768), bf16),
            pltpu.VMEM((8, 48, 384), bf16),
            pltpu.VMEM((16, 48, 6144), bf16),
            pltpu.VMEM((2, 8, 192, 768), bf16),
            pltpu.VMEM((2, 32, 24, 192), f32),
            pltpu.VMEM((2, 32, 24, 192), f32),
            pltpu.VMEM((2, 8, 24, 768), f32),
            pltpu.VMEM((2, 8, 24, 768), f32),
            dma, dma,
            dma((8,)), dma((8,)),
            dma((2, 7)), dma((2, 8)),
            dma((4, 2)), dma((4, 3, 2)), dma((16, 2)), dma((16, 2)), dma((16, 2)),
            dma((2, 32)), dma((2, 32)),
            dma((2, 8)), dma((2, 8)),
        ],
        compiler_params=pltpu.CompilerParams(
            collective_id=0, has_side_effects=True, vmem_limit_bytes=48 * 2**20),
        cost_estimate=pl.CostEstimate(flops=2 * 2 * 192 * 768 * 6144, bytes_accessed=3 * 2**20, transcendentals=0),
    )(amplitudes, driving, rloc, rowe, cole, rowi, coli)
    return jnp.where(rowi == coli, -tot / (rowe + cole), 0.0)


def solution(mesh):
    in_specs = (P("ta", "ka"), P("ta", "ka"), P("ka", "ta"), P(), P(), P(), P(), P())
    return jax.shard_map(local, mesh=mesh, in_specs=in_specs, out_specs=P("ta", "ka"), check_vma=False)
```

time: 375 us -> 195 us (0.52)
  waiting for transfers between devices: 234 us -> 0 us
  Pallas kernels: 0 us -> 181 us
  blocking collectives: 46.5 us -> 0 us
  local copies, waits for them, and re-layouts: 42.6 us -> 6.62 us
  matrix products: 18.7 us -> 0 us
  starting transfers between devices: 15.1 us -> 0 us
  between operations: 13.3 us -> 0.15 us
    pallas_call x0 -> x1, Pallas kernels: none -> 181 us  [local(): pl.pallas_call(kernel, out_shape=jax.ShapeDtypeStruct((rows, cols), f32),...]
    reduce_scatter x2 -> x0, waiting for transfers between devices: 115 us -> none  [local(): lax.psum_scatter(partial_value, 'ka', scatter_dimension=1, tiled=True)]
    all_gather x1 -> x0, waiting for transfers between devices: 90.9 us -> none  [local(): gathered = lax.all_gather(cycle_ints, 'ta', axis=1, tiled=True)]
    all_to_all x2 -> x0, blocking collectives: 46.5 us -> none  [the longest x1 30.8 us: local(): lax.all_to_all(own_cycle, 'ta', split_axis=1, concat_axis=1, tiled=True)]
    all_to_all x2 -> x0, waiting for transfers between devices: 27.4 us -> none  [the longest x1 19 us: local(): lax.all_to_all(own_cycle, 'ta', split_axis=1, concat_axis=1, tiled=True)]
    dot_general x2 -> x0, matrix products: 18.7 us -> none  [local(): partial_value = jnp.dot(operand, whole, preferred_element_type=jnp.float32)]
    transpose x3 -> x0, local copies, waits for them, and re-layouts: 16 us -> none  [the longest x2 8.04 us: local(): mirrored = received.reshape(n_ka, block, n_ta, block).transpose(0, 3, 2,...]
    all_to_all x2 -> x0, starting transfers between devices: 14.8 us -> none  [the longest x1 9.38 us: local(): lax.all_to_all(own_cycle, 'ta', split_axis=1, concat_axis=1, tiled=True)]
  transfers between devices with their start and end apart: 5 -> 0, of which waited for: 5 -> 0; matrix products, arithmetic and copies ran while one was open for 1% -> 0% of each run, Pallas kernels for 0% -> 0%
where the time goes in v1:
time: 195 us; the launch traced here: 193 us
  Pallas kernels  181 us (93%)
  local copies, waits for them, and re-layouts  6.62 us (3%)
  other arithmetic  5.64 us (3%)
    pallas_call x1, Pallas kernels, local(): pl.pallas_call(kernel, out_shape=jax.ShapeDtypeStruct((rows, cols), f32),...  181 us

profile of v1, /device:TPU:1, one launch (start us, length us, event | category | flops | bytes accessed | tf_op | source)
XLA Modules:
  0.0 193.1 jit_solution(8287137742939593764)
XLA Ops:
  0.0 0.0 copy-start
  0.0 0.9 select_reduce_fusion.1
  0.9 0.9 select_reduce_fusion
  1.8 0.1 sub.36
  1.8 0.1 sub.37
  1.9 0.6 dynamic-slice.1
  2.5 0.1 xor.33
  2.6 0.1 xor.34
  2.7 0.7 dynamic-slice
  3.3 0.8 xor.36
  4.1 0.8 sub.33
  4.9 0.7 fusion.1
  5.5 0.7 dynamic-slice_subtract_fusion.1
  6.2 0.7 fusion
  6.9 0.7 dynamic-slice_xor_fusion.1
  7.6 0.8 xor.41
  8.4 0.8 sub.40
  9.2 0.1 copy.16.rowi
  9.4 0.0 copy-start.2
  9.4 0.1 copy.15.rowe
  9.5 0.1 dynamic-slice_subtract_fusion
  9.6 0.1 reshape.46.cole
  9.7 0.1 add.33
  9.8 0.1 dynamic-slice_xor_fusion
  9.9 0.1 reshape.48.coli
  10.0 0.1 eq.35
  10.0 0.0 copy-done
  10.1 0.3 copy-done.2
  10.3 0.0 copy-start.1
  10.3 1.1 copy-done.1
  11.4 180.7 %shard_map.82 = f32[192,768]{1,0:T(8,128)S(1)} custom-call(f32[192,768]{1,0:T(8,128)S(1)} %copy-done, f32[192,768]{1,0:T(8,128)S(1)} %copy-done.1, bf16[8,24,768]{2,1,0:T(8,128)(2,1)S(1)} %bitcast.25, f32[192,1]{1,0:T(8,128)S(1)} %copy.15.rowe, f32[1,768]{1,0:T(1,128)S(1)} %reshape.46.cole, s32[192,1]{1,0:T(8,128)S(1)} %copy.16.rowi, s32[1,768]{1,0:T(1,128)S(1)} %reshape.48.coli), custom_call_target="tpu_custom_call" | custom-call | flops 3623878656 | bytes 3145728 | tf_op jit(solution)/shard_map/pallas_call | solution.py:219
  192.1 1.0 divide_select_fusion
  (6 shorter events, 0.0 us)
Async XLA Ops:
  0.0 10.0 %copy-start = (f32[192,768]{1,0:T(8,128)S(1)}, f32[192,768]{1,0:T(8,128)}, u32[]{:S(2)}) copy-start(f32[192,768]{1,0:T(8,128)} %amp.1) | copy-start | bytes 1769476
  9.4 1.0 copy-start.2
  10.3 1.1 copy-start.1

commit v2 on v0

v2 whole, which is shorter than its diff:
```python
import jax
import jax.numpy as jnp
from jax import lax
from jax.experimental import pallas as pl
from jax.experimental.pallas import tpu as pltpu
from jax.sharding import PartitionSpec as P

MESH = pl.DeviceIdType.MESH
NT = (((1,), (1,)), ((), ()))
F32, BF16 = jnp.float32, jnp.bfloat16


PIECES = ((0, 1280), (1280, 1280), (2560, 512))


def kernel(amp_h, drv_h, rloc_h, vire, viri, occe, occi, slab, out,
           amp, drv, rloc, rpair, rsend, rt, ball, bn, ct, cp, pk, u, xs, m, ch,
           l_s, s_s, p_r, a_r, b_r, r_r, c_r, cp_r, u_r, m_r):
    s = lax.axis_index("ka")
    t = lax.axis_index("ta")
    zlo, x = s // 4, s % 4
    y, zhi, core = t // 8, (t // 2) % 4, t % 2
    j = t // 2
    other = 1 - core

    loads = [pltpu.make_async_copy(rloc_h, rloc, l_s.at[0]),
             pltpu.make_async_copy(amp_h, amp, l_s.at[1]),
             pltpu.make_async_copy(drv_h, drv, l_s.at[2])]
    for copy in loads:
        copy.start()

    def dev(dy, dz):
        return (s, ((y + dy) % 4 * 4 + (zhi + dz) % 4) * 2 + core)

    zp = (1 - zlo) * 4 + x
    cpart = (s, j * 2 + other)
    greet = [((s + d) % 8, t) for d in range(1, 8)] + [cpart]
    greet += [dev(0, d) for d in (1, 2, 3)] + [dev(d, 0) for d in (1, 2, 3)]
    barrier = pltpu.get_barrier_semaphore()
    for peer in greet:
        pl.semaphore_signal(barrier, inc=1, device_id=peer, device_id_type=MESH)
    pl.semaphore_wait(barrier, len(greet))

    pending = []

    def send(src, dst, rs, peer):
        copy = pltpu.make_async_remote_copy(
            src_ref=src, dst_ref=dst, send_sem=s_s.at[len(pending)], recv_sem=rs, device_id=peer, device_id_type=MESH)
        copy.start()
        pending.append(copy)

    def arrived(dst, rs):
        pltpu.make_async_remote_copy(
            src_ref=dst, dst_ref=dst, send_sem=s_s.at[0], recv_sem=rs, device_id=cpart, device_id_type=MESH).wait_recv()

    loads[0].wait()
    send(rloc, rpair, p_r, cpart)
    loads[1].wait()
    for k in range(3):
        ball[0, k, s] = amp[k * 64:k * 64 + 64].astype(BF16)
    arrived(rpair, p_r)
    own_first = core == 0
    for q in range(8):
        a = rloc[q].astype(F32)
        b = rpair[q].astype(F32)
        both = jnp.concatenate([jnp.where(own_first, a, b), jnp.where(own_first, b, a)], axis=0).astype(BF16)
        rsend[q] = jnp.where(own_first, both[:, :384], both[:, 384:])

    def kslot(q):
        return pl.ds(pl.multiple_of(core * 3072 + q * 384, 384), 384)

    for d in range(1, 8):
        q = (s + d) % 8
        send(rsend.at[q], rt.at[j, :, kslot(s)], a_r.at[s], (q, t))
    rt[j, :, kslot(s)] = rsend[s]

    hot = lax.broadcasted_iota(jnp.int32, (1, 128), 1)

    def slab_at(i):
        here = hot == slab[i]
        return (jnp.sum(jnp.where(here, occe[...], 0.0), axis=1, keepdims=True),
                jnp.sum(jnp.where(here, occi[...], 0), axis=1, keepdims=True))

    def tile_part(v):
        runs = [jnp.concatenate([v[:, i * 192 + q * 24:i * 192 + q * 24 + 24] for i in range(8)], axis=1) for q in range(8)]
        part = runs[0]
        for q in range(1, 8):
            part = jnp.where(s == q, runs[q], part)
        return part

    def row_part(v):
        part = v[:, :192]
        for i in range(1, 8):
            part = jnp.where(t % 8 == i, v[:, i * 192:i * 192 + 192], part)
        return part

    picked = [slab_at(i) for i in range(4)]
    vce, vci = tile_part(vire[...]), tile_part(viri[...])
    cole = jnp.concatenate([vce - picked[i][0] for i in range(4)], axis=1)
    coli = jnp.concatenate([jnp.bitwise_xor(vci, picked[i][1]) for i in range(4)], axis=1)
    rowe_v, rowi_v = slab_at(y)
    rowe_l = row_part(vire[...]) - rowe_v
    rowi_l = jnp.bitwise_xor(row_part(viri[...]), rowi_v).astype(F32)

    def stand(line):
        wide = jnp.concatenate([line, jnp.zeros((1, 64), F32)], axis=1)
        return jnp.broadcast_to(wide, (128, 256)).T[:192, :1]

    rowe = stand(rowe_l).reshape(8, 24, 1)
    rowi = stand(rowi_l).reshape(8, 24, 1)
    coli = coli.astype(F32)

    for d in range(1, 8):
        q = (s + d) % 8
        arrived(rt.at[j, :, kslot(q)], a_r.at[q])

    def piece(jj, p, c):
        start, size = PIECES[p]
        return rt.at[jj, :, pl.ds(pl.multiple_of(c * 3072 + start, 128), size)]

    def ahead(jj, p, peer):
        send(piece(jj, p, core), piece(jj, p, core), r_r.at[jj, p], peer)

    def to_core(jj, p):
        send(piece(jj, p, core), piece(jj, p, core), c_r.at[jj, p], cpart)

    def event(dy, dz, p):
        jj = (y + dy) % 4 * 4 + (zhi + dz) % 4
        arrived(piece(jj, p, core), r_r.at[jj, p])
        if p < 2:
            if dy == 0:
                if (dz, p) == (3, 0):
                    ahead(jj, p, dev(0, 1))
                if (dz, p) == (1, 1):
                    ahead(jj, p, dev(0, 3))
                ahead(jj, p, dev(1, 0))
                ahead(jj, p, dev(3, 0))
            if (dy, p) == (3, 0):
                ahead(jj, p, dev(1, 0))
            if (dy, p) == (1, 1):
                ahead(jj, p, dev(3, 0))
        elif dz == 0:
            for d in (1, 3, 2):
                ahead(jj, p, dev(0, d))
        to_core(jj, p)

    def bpart(it, k, q, h):
        return ball.at[it, k, q, h * 32:h * 32 + 32]

    def b_to(it, k, q, h, peer):
        send(bpart(it, k, q, h), bpart(it, k, q, h), b_r.at[it, k, q, h], (peer, t))

    def b_at(it, k, q, h):
        arrived(bpart(it, k, q, h), b_r.at[it, k, q, h])

    def round_x(d):
        return zlo * 4 + (x + d) % 4

    def spread_b(it, k):
        for h in (0, 1):
            b_to(it, k, s, h, zp)
        for h in (0, 1):
            b_to(it, k, s, h, round_x(1))
            b_to(it, k, s, h, round_x(3))

    def partner_b(it, k):
        for h in (0, 1):
            b_at(it, k, zp, h)
            b_to(it, k, zp, h, round_x(1))
            b_to(it, k, zp, h, round_x(3))

    def onward_b(it, k, z):
        left = (zlo + z) % 2 * 4 + (x + 3) % 4
        right = (zlo + z) % 2 * 4 + (x + 1) % 4
        b_at(it, k, left, 0)
        b_to(it, k, left, 0, round_x(1))
        b_at(it, k, right, 0)
        b_at(it, k, left, 1)
        b_at(it, k, right, 1)
        b_to(it, k, right, 1, round_x(3))

    def last_b(it, k):
        for z in (0, 1):
            for h in (0, 1):
                b_at(it, k, (zlo + z) % 2 * 4 + (x + 2) % 4, h)

    for p in (0, 1):
        ahead(j, p, dev(0, 1))
        ahead(j, p, dev(0, 3))
        ahead(j, p, dev(1, 0))
        ahead(j, p, dev(3, 0))
    for d in (1, 3, 2):
        ahead(j, 2, dev(d, 0))
    for k in range(3):
        spread_b(0, k)
    for p in (0, 1, 2):
        to_core(j, p)
    for p in (0, 1):
        for d in (3, 1):
            event(0, d, p)
            event(d, 0, p)
    for d in (1, 3, 2):
        ahead(j, 2, dev(0, d))
    for k in range(3):
        onward_b(0, k, 0)
    event(1, 0, 2)
    event(3, 0, 2)
    for p in (0, 1):
        event(0, 2, p)
        event(2, 0, p)
    event(2, 0, 2)
    for k in range(3):
        partner_b(0, k)
    for p in (0, 1):
        for dz in (3, 1):
            for dy in (3, 1):
                event(dy, dz, p)
    for k in range(3):
        onward_b(0, k, 1)
    for p in (0, 1):
        for dy in (3, 1):
            event(dy, 2, p)
    for p in (0, 1):
        for dz in (3, 1):
            event(2, dz, p)
    for dz in (1, 3, 2):
        for dy in (0, 1, 3, 2):
            event(dy, dz, 2)
    for p in (0, 1):
        event(2, 2, p)
    for k in range(3):
        last_b(0, k)
    for dy in (0, 1, 3, 2):
        for dz in (0, 1, 3, 2):
            jj = (y + dy) % 4 * 4 + (zhi + dz) % 4
            for p in (0, 1, 2):
                arrived(piece(jj, p, other), c_r.at[jj, p])

    def cycle(it, rhs):
        slabs = [(y + d) % 4 for d in (2, 1, 3, 0)]
        for yy in slabs:
            left = rt[pl.ds(yy * 4, 4)].reshape(192, 6144)
            acc = lax.dot_general(left, rhs(), NT, preferred_element_type=F32).reshape(4, 2, 24, 192)
            ct[it, 0, pl.ds(yy * 4, 4)] = acc[:, 0]
            ct[it, 1, pl.ds(yy * 4, 4)] = acc[:, 1]
            send(ct.at[it, other, pl.ds(yy * 4, 4)], cp.at[it, pl.ds(yy * 4, 4)], cp_r.at[it, yy], cpart)
        for yy in slabs:
            arrived(cp.at[it, pl.ds(yy * 4, 4)], cp_r.at[it, yy])
            for i in range(4):
                mine, theirs = ct[it, core, yy * 4 + i], cp[it, yy * 4 + i]
                pk[it, yy * 4 + i] = jnp.concatenate(
                    [jnp.where(own_first, mine, theirs), jnp.where(own_first, theirs, mine)], axis=1)
        for c in range(3):
            rows = slice(c * 8, c * 8 + 8)
            for dz in (2, 1, 3, 0):
                for dy in (2, 1, 3, 0):
                    if dy + dz:
                        jj = (y + dy) % 4 * 4 + (zhi + dz) % 4
                        send(pk.at[it, jj, rows], u.at[it, j, rows], u_r.at[it, j, c], dev(dy, dz))
        u[it, j] = pk[it, j]
        square = jnp.concatenate([ct[it, i % 2, i // 2] for i in range(32)], axis=0)
        square = jnp.concatenate([square, jnp.zeros((768, 64), F32)], axis=1).T[:192]
        ch[...] = square + drv[...]

    def mirror(it, c):
        rows = slice(c * 8, c * 8 + 8)
        for dy in (0, 1, 3, 2):
            for dz in (0, 1, 3, 2):
                if dy + dz:
                    jj = (y + dy) % 4 * 4 + (zhi + dz) % 4
                    arrived(u.at[it, jj, rows], u_r.at[it, jj, c])
        for q in range(8):
            xs[it, q, rows] = jnp.concatenate(
                [u[it, i // 2, rows, i % 2 * 192 + q * 24:i % 2 * 192 + q * 24 + 24] for i in range(32)], axis=1)
        for d in (2, 6, 1, 3, 5, 7, 4):
            q = (s + d) % 8
            send(xs.at[it, q, rows], m.at[it, s, rows], m_r.at[it, s, c], (q, t))
        m[it, s, rows] = xs[it, s, rows]

    def update(it, c):
        rows = slice(c * 8, c * 8 + 8)
        for d in range(1, 8):
            q = (s + d) % 8
            arrived(m.at[it, q, rows], m_r.at[it, q, c])
        tot = ch[...].reshape(8, 24, 768)[:, rows] + m[it, :, rows]
        keep = rowi[:, rows] == coli.reshape(1, 1, 768)
        return jnp.where(keep, -tot / (rowe[:, rows] + cole.reshape(1, 1, 768)), 0.0)

    def next_b(c):
        ball[1, c, s] = update(0, c).reshape(64, 768).astype(BF16)
        spread_b(1, c)

    def first_rhs():
        return jnp.concatenate([jnp.concatenate([ball[0, k, q, :, h * 384:h * 384 + 384] for k in range(3)], axis=0)
                                for h in (0, 1) for q in range(8)], axis=1)

    def second_rhs():
        return jnp.concatenate([bn[q, :, h * 384:h * 384 + 384] for h in (0, 1) for q in range(8)], axis=1)

    loads[2].wait()
    cycle(0, first_rhs)
    mirror(0, 0)
    mirror(0, 1)
    next_b(0)
    mirror(0, 2)
    next_b(1)
    onward_b(1, 0, 0)
    partner_b(1, 0)
    next_b(2)
    onward_b(1, 1, 0)
    partner_b(1, 1)
    onward_b(1, 0, 1)
    onward_b(1, 2, 0)
    partner_b(1, 2)
    onward_b(1, 1, 1)
    onward_b(1, 2, 1)
    for k in range(3):
        last_b(1, k)
    for q in range(8):
        thirds = [ball[1, k, q].astype(F32).reshape(8, 8, 768) for k in range(3)]
        bn[q] = jnp.concatenate([thirds[i % 3][i // 3] for i in range(24)], axis=0).astype(BF16)
    cycle(1, second_rhs)
    for c in range(3):
        mirror(1, c)
    for c in range(3):
        out[:, c * 8:c * 8 + 8] = update(1, c)
    for copy in pending:
        copy.wait_send()


def local(amplitudes, driving, cycle_ints, occ_irrep, vir_irrep, occ_energy, vir_energy, slab):
    rows, cols = amplitudes.shape
    rloc = cycle_ints.T.reshape(8, 24, cols)
    dma = pltpu.SemaphoreType.DMA
    vmem = pl.BlockSpec(memory_space=pltpu.VMEM)
    result = pl.pallas_call(
        kernel,
        out_shape=jax.ShapeDtypeStruct((8, 24, cols), F32),
        in_specs=[pl.BlockSpec(memory_space=pl.ANY)] * 3 + [vmem] * 4 + [pl.BlockSpec(memory_space=pltpu.SMEM)],
        out_specs=vmem,
        scratch_shapes=[
            pltpu.VMEM((192, 768), F32),
            pltpu.VMEM((192, 768), F32),
            pltpu.VMEM((8, 24, 768), BF16),
            pltpu.VMEM((8, 24, 768), BF16),
            pltpu.VMEM((8, 48, 384), BF16),
            pltpu.VMEM((16, 48, 6144), BF16),
            pltpu.VMEM((2, 3, 8, 64, 768), BF16),
            pltpu.VMEM((8, 192, 768), BF16),
            pltpu.VMEM((2, 2, 16, 24, 192), F32),
            pltpu.VMEM((2, 16, 24, 192), F32),
            pltpu.VMEM((2, 16, 24, 384), F32),
            pltpu.VMEM((2, 16, 24, 384), F32),
            pltpu.VMEM((2, 8, 24, 768), F32),
            pltpu.VMEM((2, 8, 24, 768), F32),
            pltpu.VMEM((192, 768), F32),
            dma((3,)), dma((512,)), dma, dma((8,)), dma((2, 3, 8, 2)), dma((16, 3)), dma((16, 3)), dma((2, 4)),
            dma((2, 16, 3)), dma((2, 8, 3)),
        ],
        compiler_params=pltpu.CompilerParams(
            collective_id=0, has_side_effects=True, vmem_limit_bytes=48 * 2**20),
        cost_estimate=pl.CostEstimate(flops=2 * 2 * 192 * 768 * 6144, bytes_accessed=3 * 2**20, transcendentals=0),
    )(amplitudes, driving, rloc, vir_energy.reshape(1, -1), vir_irrep.reshape(1, -1),
      occ_energy.reshape(1, -1), occ_irrep.reshape(1, -1), slab)
    return result.reshape(rows, cols)


def solution(mesh):
    in_specs = (P("ta", "ka"), P("ta", "ka"), P("ka", "ta"), P(), P(), P(), P(), P())
    return jax.shard_map(local, mesh=mesh, in_specs=in_specs, out_specs=P("ta", "ka"), check_vma=False)
```

time: 375 us -> 154 us (0.41)
  waiting for transfers between devices: 234 us -> 0 us
  Pallas kernels: 0 us -> 148 us
  blocking collectives: 46.5 us -> 0 us
  local copies, waits for them, and re-layouts: 42.6 us -> 5.28 us
  matrix products: 18.7 us -> 0 us
  starting transfers between devices: 15.1 us -> 0 us
  between operations: 13.3 us -> 0.04 us
  other arithmetic: 4.1 us -> 0 us
    pallas_call x0 -> x1, Pallas kernels: none -> 148 us  [local(): pl.pallas_call(kernel, out_shape=jax.ShapeDtypeStruct((8, 24, cols), F32)...]
    reduce_scatter x2 -> x0, waiting for transfers between devices: 115 us -> none  [local(): lax.psum_scatter(partial_value, 'ka', scatter_dimension=1, tiled=True)]
    all_gather x1 -> x0, waiting for transfers between devices: 90.9 us -> none  [local(): gathered = lax.all_gather(cycle_ints, 'ta', axis=1, tiled=True)]
    all_to_all x2 -> x0, blocking collectives: 46.5 us -> none  [the longest x1 30.8 us: local(): lax.all_to_all(own_cycle, 'ta', split_axis=1, concat_axis=1, tiled=True)]
    all_to_all x2 -> x0, waiting for transfers between devices: 27.4 us -> none  [the longest x1 19 us: local(): lax.all_to_all(own_cycle, 'ta', split_axis=1, concat_axis=1, tiled=True)]
    dot_general x2 -> x0, matrix products: 18.7 us -> none  [local(): partial_value = jnp.dot(operand, whole, preferred_element_type=jnp.float32)]
    transpose x3 -> x0, local copies, waits for them, and re-layouts: 16 us -> none  [the longest x2 8.04 us: local(): mirrored = received.reshape(n_ka, block, n_ta, block).transpose(0, 3, 2,...]
    all_to_all x2 -> x0, starting transfers between devices: 14.8 us -> none  [the longest x1 9.38 us: local(): lax.all_to_all(own_cycle, 'ta', split_axis=1, concat_axis=1, tiled=True)]
  transfers between devices with their start and end apart: 5 -> 0, of which waited for: 5 -> 0; matrix products, arithmetic and copies ran while one was open for 1% -> 0% of each run, Pallas kernels for 0% -> 0%
where the time goes in v2:
time: 154 us; the launch traced here: 153 us
  Pallas kernels  148 us (96%)
  local copies, waits for them, and re-layouts  5.28 us (3%)
    pallas_call x1, Pallas kernels, local(): pl.pallas_call(kernel, out_shape=jax.ShapeDtypeStruct((8, 24, cols), F32)...  148 us
    unnamed x15, local copies, waits for them, and re-layouts  4.56 us

profile of v2, /device:TPU:1, one launch (start us, length us, event | category | flops | bytes accessed | tf_op | source)
XLA Modules:
  0.0 153.4 jit_solution(14753629563060628169)
XLA Ops:
  0.0 0.0 copy-start.6
  0.0 0.7 reshape.20.viri
  0.7 0.0 copy-done.6
  0.7 0.0 copy-start.3
  0.7 0.0 copy-start.4
  0.7 0.0 copy-start.5
  0.8 0.6 copy-done.3
  1.4 0.0 copy-done.4
  1.4 0.0 copy-done.5
  1.4 0.0 copy-start
  1.4 1.1 copy-done
  2.5 0.0 copy-start.1
  2.5 1.1 copy-done.1
  3.5 0.0 copy-start.2
  3.5 1.0 copy-done.2
  4.5 148.0 %shard_map.82 = f32[8,24,768]{2,1,0:T(8,128)S(1)} custom-call(f32[192,768]{1,0:T(8,128)S(1)} %copy-done, f32[192,768]{1,0:T(8,128)S(1)} %copy-done.1, bf16[8,24,768]{2,1,0:T(8,128)(2,1)S(1)} %bitcast.7, f32[1,1536]{1,0:T(1,128)S(1)} %reshape.19.vire, s32[1,1536]{1,0:T(1,128)S(1)} %reshape.20.viri, f32[1,128]{1,0:T(1,128)S(1)} %bitcast.8, ...), custom_call_target="tpu_custom_call" | custom-call | flops 3623878656 | bytes 3145728 | tf_op jit(solution)/shard_map/pallas_call | solution.py:336
  152.6 0.8 copy.10
  (1 shorter events, 0.0 us)
Async XLA Ops:
  0.0 0.7 copy-start.6
  0.7 0.7 copy-start.3
  0.7 0.7 copy-start.4
  0.7 0.7 copy-start.5
  1.4 1.1 copy-start
  2.5 1.1 copy-start.1
  3.5 1.0 copy-start.2

commit v3 on v2

--- a/solution.py
+++ b/solution.py
@@ -10,12 +10,12 @@
 F32, BF16 = jnp.float32, jnp.bfloat16
 
 
-PIECES = ((0, 1280), (1280, 1280), (2560, 512))
+PIECES = ((0, 1408), (1408, 1280), (2688, 384))
 
 
 def kernel(amp_h, drv_h, rloc_h, vire, viri, occe, occi, slab, out,
            amp, drv, rloc, rpair, rsend, rt, ball, bn, ct, cp, pk, u, xs, m, ch,
-           l_s, s_s, p_r, a_r, b_r, r_r, c_r, cp_r, u_r, m_r):
+           l_s, p_s, p_r, a_s, a_r, g_s, r_r, c_s, c_r, b_s, b0_r, b1_r, cp_s, cp_r, u_s, u_r, m_s, m_r):
     s = lax.axis_index("ka")
     t = lax.axis_index("ta")
     zlo, x = s // 4, s % 4
@@ -34,27 +34,26 @@
 
     zp = (1 - zlo) * 4 + x
     cpart = (s, j * 2 + other)
-    greet = [((s + d) % 8, t) for d in range(1, 8)] + [cpart]
-    greet += [dev(0, d) for d in (1, 2, 3)] + [dev(d, 0) for d in (1, 2, 3)]
+    greet = [dev(0, 1), dev(0, 3), dev(1, 0), dev(3, 0)] + [((s + d) % 8, t) for d in (2, 6, 1, 3, 5, 7, 4)] + [cpart]
     barrier = pltpu.get_barrier_semaphore()
     for peer in greet:
         pl.semaphore_signal(barrier, inc=1, device_id=peer, device_id_type=MESH)
     pl.semaphore_wait(barrier, len(greet))
 
-    pending = []
-
-    def send(src, dst, rs, peer):
-        copy = pltpu.make_async_remote_copy(
-            src_ref=src, dst_ref=dst, send_sem=s_s.at[len(pending)], recv_sem=rs, device_id=peer, device_id_type=MESH)
-        copy.start()
-        pending.append(copy)
+    def send(src, dst, ss, rs, peer):
+        pltpu.make_async_remote_copy(
+            src_ref=src, dst_ref=dst, send_sem=ss, recv_sem=rs, device_id=peer, device_id_type=MESH).start()
 
     def arrived(dst, rs):
         pltpu.make_async_remote_copy(
-            src_ref=dst, dst_ref=dst, send_sem=s_s.at[0], recv_sem=rs, device_id=cpart, device_id_type=MESH).wait_recv()
+            src_ref=dst, dst_ref=dst, send_sem=p_s, recv_sem=rs, device_id=cpart, device_id_type=MESH).wait_recv()
+
+    def sent(src, ss):
+        pltpu.make_async_remote_copy(
+            src_ref=src, dst_ref=src, send_sem=ss, recv_sem=p_r, device_id=cpart, device_id_type=MESH).wait_send()
 
     loads[0].wait()
-    send(rloc, rpair, p_r, cpart)
+    send(rloc, rpair, p_s, p_r, cpart)
     loads[1].wait()
     for k in range(3):
         ball[0, k, s] = amp[k * 64:k * 64 + 64].astype(BF16)
@@ -71,7 +70,7 @@
 
     for d in range(1, 8):
         q = (s + d) % 8
-        send(rsend.at[q], rt.at[j, :, kslot(s)], a_r.at[s], (q, t))
+        send(rsend.at[q], rt.at[j, :, kslot(s)], a_s, a_r, (q, t))
     rt[j, :, kslot(s)] = rsend[s]
 
     hot = lax.broadcasted_iota(jnp.int32, (1, 128), 1)
@@ -110,19 +109,17 @@
     rowi = stand(rowi_l).reshape(8, 24, 1)
     coli = coli.astype(F32)
 
-    for d in range(1, 8):
-        q = (s + d) % 8
-        arrived(rt.at[j, :, kslot(q)], a_r.at[q])
+    arrived(rsend.at[0:7], a_r)
 
     def piece(jj, p, c):
         start, size = PIECES[p]
         return rt.at[jj, :, pl.ds(pl.multiple_of(c * 3072 + start, 128), size)]
 
     def ahead(jj, p, peer):
-        send(piece(jj, p, core), piece(jj, p, core), r_r.at[jj, p], peer)
+        send(piece(jj, p, core), piece(jj, p, core), g_s, r_r.at[jj, p], peer)
 
     def to_core(jj, p):
-        send(piece(jj, p, core), piece(jj, p, core), c_r.at[jj, p], cpart)
+        send(piece(jj, p, core), piece(jj, p, core), c_s, c_r, cpart)
 
     def event(dy, dz, p):
         jj = (y + dy) % 4 * 4 + (zhi + dz) % 4
@@ -144,79 +141,88 @@
                 ahead(jj, p, dev(0, d))
         to_core(jj, p)
 
-    def bpart(it, k, q, h):
-        return ball.at[it, k, q, h * 32:h * 32 + 32]
-
-    def b_to(it, k, q, h, peer):
-        send(bpart(it, k, q, h), bpart(it, k, q, h), b_r.at[it, k, q, h], (peer, t))
-
-    def b_at(it, k, q, h):
-        arrived(bpart(it, k, q, h), b_r.at[it, k, q, h])
+    def bpart(k, q, h):
+        rows = slice(h * 32, h * 32 + 32)
+        return (ball.at[0, :, q, rows], b0_r.at[q, h]) if k is None else (ball.at[1, k, q, rows], b1_r.at[k, q, h])
+
+    def b_to(k, q, h, peer):
+        ref, sem = bpart(k, q, h)
+        send(ref, ref, b_s.at[0 if k is None else 1], sem, (peer, t))
+
+    def b_at(k, q, h):
+        arrived(*bpart(k, q, h))
 
     def round_x(d):
         return zlo * 4 + (x + d) % 4
 
-    def spread_b(it, k):
+    def spread_b(k):
         for h in (0, 1):
-            b_to(it, k, s, h, zp)
+            b_to(k, s, h, zp)
         for h in (0, 1):
-            b_to(it, k, s, h, round_x(1))
-            b_to(it, k, s, h, round_x(3))
-
-    def partner_b(it, k):
+            b_to(k, s, h, round_x(1))
+            b_to(k, s, h, round_x(3))
+
+    def partner_b(k):
         for h in (0, 1):
-            b_at(it, k, zp, h)
-            b_to(it, k, zp, h, round_x(1))
-            b_to(it, k, zp, h, round_x(3))
-
-    def onward_b(it, k, z):
+            b_at(k, zp, h)
+            b_to(k, zp, h, round_x(1))
+            b_to(k, zp, h, round_x(3))
+
+    def onward_b(k, z, cross=False):
         left = (zlo + z) % 2 * 4 + (x + 3) % 4
         right = (zlo + z) % 2 * 4 + (x + 1) % 4
-        b_at(it, k, left, 0)
-        b_to(it, k, left, 0, round_x(1))
-        b_at(it, k, right, 0)
-        b_at(it, k, left, 1)
-        b_at(it, k, right, 1)
-        b_to(it, k, right, 1, round_x(3))
-
-    def last_b(it, k):
+        for q, h in ((left, 0), (right, 1), (left, 1), (right, 0)):
+            b_at(k, q, h)
+            if (q is left) == (h == 0):
+                b_to(k, q, h, round_x(1) if q is left else round_x(3))
+            if cross:
+                b_to(k, q, h, zp)
+
+    def last_b(k):
         for z in (0, 1):
             for h in (0, 1):
-                b_at(it, k, (zlo + z) % 2 * 4 + (x + 2) % 4, h)
+                b_at(k, (zlo + z) % 2 * 4 + (x + 2) % 4, h)
+
+    def cross_b(k):
+        for h in (0, 1):
+            b_at(k, round_x(2), h)
+            b_to(k, round_x(2), h, zp)
+
+    def crossed_b(k):
+        for d in range(4):
+            for h in (0, 1):
+                b_at(k, (1 - zlo) * 4 + (x + d) % 4, h)
 
     for p in (0, 1):
         ahead(j, p, dev(0, 1))
         ahead(j, p, dev(0, 3))
         ahead(j, p, dev(1, 0))
         ahead(j, p, dev(3, 0))
-    for d in (1, 3, 2):
+    for d in (1, 3):
         ahead(j, 2, dev(d, 0))
-    for k in range(3):
-        spread_b(0, k)
+    spread_b(None)
     for p in (0, 1, 2):
         to_core(j, p)
     for p in (0, 1):
         for d in (3, 1):
             event(0, d, p)
             event(d, 0, p)
+    ahead(j, 2, dev(2, 0))
     for d in (1, 3, 2):
         ahead(j, 2, dev(0, d))
-    for k in range(3):
-        onward_b(0, k, 0)
+    onward_b(None, 0)
     event(1, 0, 2)
     event(3, 0, 2)
     for p in (0, 1):
         event(0, 2, p)
         event(2, 0, p)
     event(2, 0, 2)
-    for k in range(3):
-        partner_b(0, k)
+    partner_b(None)
     for p in (0, 1):
         for dz in (3, 1):
             for dy in (3, 1):
                 event(dy, dz, p)
-    for k in range(3):
-        onward_b(0, k, 1)
+    onward_b(None, 1)
     for p in (0, 1):
         for dy in (3, 1):
             event(dy, 2, p)
@@ -228,35 +234,44 @@
             event(dy, dz, 2)
     for p in (0, 1):
         event(2, 2, p)
-    for k in range(3):
-        last_b(0, k)
-    for dy in (0, 1, 3, 2):
-        for dz in (0, 1, 3, 2):
-            jj = (y + dy) % 4 * 4 + (zhi + dz) % 4
-            for p in (0, 1, 2):
-                arrived(piece(jj, p, other), c_r.at[jj, p])
+    last_b(None)
+    arrived(rt.at[:, :, pl.ds(pl.multiple_of(other * 3072, 3072), 3072)], c_r)
 
     def cycle(it, rhs):
-        slabs = [(y + d) % 4 for d in (2, 1, 3, 0)]
-        for yy in slabs:
+        steps = (2, 1, 3, 0)
+        slabs = [(y + d) % 4 for d in steps]
+
+        def product(yy):
             left = rt[pl.ds(yy * 4, 4)].reshape(192, 6144)
             acc = lax.dot_general(left, rhs(), NT, preferred_element_type=F32).reshape(4, 2, 24, 192)
             ct[it, 0, pl.ds(yy * 4, 4)] = acc[:, 0]
             ct[it, 1, pl.ds(yy * 4, 4)] = acc[:, 1]
-            send(ct.at[it, other, pl.ds(yy * 4, 4)], cp.at[it, pl.ds(yy * 4, 4)], cp_r.at[it, yy], cpart)
-        for yy in slabs:
+            send(ct.at[it, other, pl.ds(yy * 4, 4)], cp.at[it, pl.ds(yy * 4, 4)], cp_s.at[it], cp_r.at[it, yy], cpart)
+
+        def to_mirror(dy, c):
+            rows = slice(c * 8, c * 8 + 8)
+            for dz in (2, 1, 3, 0):
+                if dy + dz:
+                    jj = (y + dy) % 4 * 4 + (zhi + dz) % 4
+                    send(pk.at[it, jj, rows], u.at[it, j, rows], u_s.at[it], u_r.at[it, c], dev(dy, dz))
+
+        def pack(g):
+            yy = slabs[g]
             arrived(cp.at[it, pl.ds(yy * 4, 4)], cp_r.at[it, yy])
             for i in range(4):
                 mine, theirs = ct[it, core, yy * 4 + i], cp[it, yy * 4 + i]
                 pk[it, yy * 4 + i] = jnp.concatenate(
                     [jnp.where(own_first, mine, theirs), jnp.where(own_first, theirs, mine)], axis=1)
-        for c in range(3):
-            rows = slice(c * 8, c * 8 + 8)
-            for dz in (2, 1, 3, 0):
-                for dy in (2, 1, 3, 0):
-                    if dy + dz:
-                        jj = (y + dy) % 4 * 4 + (zhi + dz) % 4
-                        send(pk.at[it, jj, rows], u.at[it, j, rows], u_r.at[it, j, c], dev(dy, dz))
+            to_mirror(steps[g], 0)
+
+        product(slabs[0])
+        for g in range(1, 4):
+            product(slabs[g])
+            pack(g - 1)
+        pack(3)
+        for c in (1, 2):
+            for dy in steps:
+                to_mirror(dy, c)
         u[it, j] = pk[it, j]
         square = jnp.concatenate([ct[it, i % 2, i // 2] for i in range(32)], axis=0)
         square = jnp.concatenate([square, jnp.zeros((768, 64), F32)], axis=1).T[:192]
@@ -264,31 +279,25 @@
 
     def mirror(it, c):
         rows = slice(c * 8, c * 8 + 8)
-        for dy in (0, 1, 3, 2):
-            for dz in (0, 1, 3, 2):
-                if dy + dz:
-                    jj = (y + dy) % 4 * 4 + (zhi + dz) % 4
-                    arrived(u.at[it, jj, rows], u_r.at[it, jj, c])
+        arrived(u.at[it, 0:15, rows], u_r.at[it, c])
         for q in range(8):
             xs[it, q, rows] = jnp.concatenate(
                 [u[it, i // 2, rows, i % 2 * 192 + q * 24:i % 2 * 192 + q * 24 + 24] for i in range(32)], axis=1)
         for d in (2, 6, 1, 3, 5, 7, 4):
             q = (s + d) % 8
-            send(xs.at[it, q, rows], m.at[it, s, rows], m_r.at[it, s, c], (q, t))
+            send(xs.at[it, q, rows], m.at[it, s, rows], m_s.at[it], m_r.at[it, c], (q, t))
         m[it, s, rows] = xs[it, s, rows]
 
     def update(it, c):
         rows = slice(c * 8, c * 8 + 8)
-        for d in range(1, 8):
-            q = (s + d) % 8
-            arrived(m.at[it, q, rows], m_r.at[it, q, c])
+        arrived(m.at[it, 0:7, rows], m_r.at[it, c])
         tot = ch[...].reshape(8, 24, 768)[:, rows] + m[it, :, rows]
         keep = rowi[:, rows] == coli.reshape(1, 1, 768)
         return jnp.where(keep, -tot / (rowe[:, rows] + cole.reshape(1, 1, 768)), 0.0)
 
     def next_b(c):
         ball[1, c, s] = update(0, c).reshape(64, 768).astype(BF16)
-        spread_b(1, c)
+        spread_b(c)
 
     def first_rhs():
         return jnp.concatenate([jnp.concatenate([ball[0, k, q, :, h * 384:h * 384 + 384] for k in range(3)], axis=0)
@@ -304,18 +313,18 @@
     next_b(0)
     mirror(0, 2)
     next_b(1)
-    onward_b(1, 0, 0)
-    partner_b(1, 0)
+    onward_b(0, 0)
+    partner_b(0)
     next_b(2)
-    onward_b(1, 1, 0)
-    partner_b(1, 1)
-    onward_b(1, 0, 1)
-    onward_b(1, 2, 0)
-    partner_b(1, 2)
-    onward_b(1, 1, 1)
-    onward_b(1, 2, 1)
-    for k in range(3):
-        last_b(1, k)
+    onward_b(1, 0, cross=True)
+    cross_b(1)
+    onward_b(0, 1)
+    onward_b(2, 0)
+    partner_b(2)
+    onward_b(2, 1)
+    last_b(0)
+    crossed_b(1)
+    last_b(2)
     for q in range(8):
         thirds = [ball[1, k, q].astype(F32).reshape(8, 8, 768) for k in range(3)]
         bn[q] = jnp.concatenate([thirds[i % 3][i // 3] for i in range(24)], axis=0).astype(BF16)
@@ -324,8 +333,15 @@
         mirror(1, c)
     for c in range(3):
         out[:, c * 8:c * 8 + 8] = update(1, c)
-    for copy in pending:
-        copy.wait_send()
+    sent(rloc, p_s)
+    sent(rsend.at[0:7], a_s)
+    sent(rt.at[0:15, :, 0:3072], g_s)
+    sent(rt.at[:, :, 0:3072], c_s)
+    for it in (0, 1):
+        sent(ball.at[it, :, 0:7], b_s.at[it])
+        sent(cp.at[it], cp_s.at[it])
+        sent(pk.at[it, 0:15], u_s.at[it])
+        sent(xs.at[it, 0:7], m_s.at[it])
 
 
 def local(amplitudes, driving, cycle_ints, occ_irrep, vir_irrep, occ_energy, vir_energy, slab):
@@ -336,7 +352,7 @@
     result = pl.pallas_call(
         kernel,
         out_shape=jax.ShapeDtypeStruct((8, 24, cols), F32),
-        in_specs=[pl.BlockSpec(memory_space=pl.ANY)] * 3 + [vmem] * 4 + [pl.BlockSpec(memory_space=pltpu.SMEM)],
+        in_specs=[pl.BlockSpec(memory_space=pltpu.HBM)] * 3 + [vmem] * 4 + [pl.BlockSpec(memory_space=pltpu.SMEM)],
         out_specs=vmem,
         scratch_shapes=[
             pltpu.VMEM((192, 768), F32),
@@ -354,8 +370,8 @@
             pltpu.VMEM((2, 8, 24, 768), F32),
             pltpu.VMEM((2, 8, 24, 768), F32),
             pltpu.VMEM((192, 768), F32),
-            dma((3,)), dma((512,)), dma, dma((8,)), dma((2, 3, 8, 2)), dma((16, 3)), dma((16, 3)), dma((2, 4)),
-            dma((2, 16, 3)), dma((2, 8, 3)),
+            dma((3,)), dma, dma, dma, dma, dma, dma((16, 3)), dma, dma, dma((2,)), dma((8, 2)), dma((3, 8, 2)),
+            dma((2,)), dma((2, 4)), dma((2,)), dma((2, 3)), dma((2,)), dma((2, 3)),
         ],
         compiler_params=pltpu.CompilerParams(
             collective_id=0, has_side_effects=True, vmem_limit_bytes=48 * 2**20),

time: 154 us -> 141 us (0.916)
  Pallas kernels: 148 us -> 135 us
    pallas_call x1, Pallas kernels: 148 us -> 135 us  [local(): pl.pallas_call(kernel, out_shape=jax.ShapeDtypeStruct((8, 24, cols), F32)...]
where the time goes in v3:
time: 141 us; the launch traced here: 140 us
  Pallas kernels  135 us (96%)
  local copies, waits for them, and re-layouts  5.28 us (4%)
    pallas_call x1, Pallas kernels, local(): pl.pallas_call(kernel, out_shape=jax.ShapeDtypeStruct((8, 24, cols), F32)...  135 us
    unnamed x15, local copies, waits for them, and re-layouts  4.56 us

profile of v3, /device:TPU:1, one launch (start us, length us, event | category | flops | bytes accessed | tf_op | source)
XLA Modules:
  0.0 140.5 jit_solution(2023034533089438520)
XLA Ops:
  0.0 0.0 copy-start.6
  0.0 0.7 reshape.20.viri
  0.7 0.0 copy-done.6
  0.7 0.0 copy-start.3
  0.7 0.0 copy-start.4
  0.7 0.0 copy-start.5
  0.8 0.6 copy-done.3
  1.4 0.0 copy-done.4
  1.4 0.0 copy-done.5
  1.4 0.0 copy-start
  1.4 1.1 copy-done
  2.5 0.0 copy-start.1
  2.5 1.1 copy-done.1
  3.5 0.0 copy-start.2
  3.5 1.0 copy-done.2
  4.5 135.1 %shard_map.82 = f32[8,24,768]{2,1,0:T(8,128)S(1)} custom-call(f32[192,768]{1,0:T(8,128)S(1)} %copy-done, f32[192,768]{1,0:T(8,128)S(1)} %copy-done.1, bf16[8,24,768]{2,1,0:T(8,128)(2,1)S(1)} %bitcast.7, f32[1,1536]{1,0:T(1,128)S(1)} %reshape.19.vire, s32[1,1536]{1,0:T(1,128)S(1)} %reshape.20.viri, f32[1,128]{1,0:T(1,128)S(1)} %bitcast.8, ...), custom_call_target="tpu_custom_call" | custom-call | flops 3623878656 | bytes 3145728 | tf_op jit(solution)/shard_map/pallas_call | solution.py:352
  139.6 0.8 copy.10
  (1 shorter events, 0.0 us)
Async XLA Ops:
  0.0 0.7 copy-start.6
  0.7 0.7 copy-start.3
  0.7 0.7 copy-start.4
  0.7 0.7 copy-start.5
  1.4 1.1 copy-start
  2.5 1.1 copy-start.1
  3.5 1.0 copy-start.2

commit v4 on v3

--- a/solution.py
+++ b/solution.py
@@ -119,7 +119,7 @@
         send(piece(jj, p, core), piece(jj, p, core), g_s, r_r.at[jj, p], peer)
 
     def to_core(jj, p):
-        send(piece(jj, p, core), piece(jj, p, core), c_s, c_r, cpart)
+        send(piece(jj, p, core), piece(jj, p, core), c_s, c_r.at[jj // 4], cpart)
 
     def event(dy, dz, p):
         jj = (y + dy) % 4 * 4 + (zhi + dz) % 4
@@ -193,6 +193,49 @@
             for h in (0, 1):
                 b_at(k, (1 - zlo) * 4 + (x + d) % 4, h)
 
+    def product(it, dy, rhs):
+        yy = (y + dy) % 4
+        left = rt[pl.ds(yy * 4, 4)].reshape(192, 6144)
+        acc = lax.dot_general(left, rhs(), NT, preferred_element_type=F32).reshape(4, 2, 24, 192)
+        ct[it, 0, pl.ds(yy * 4, 4)] = acc[:, 0]
+        ct[it, 1, pl.ds(yy * 4, 4)] = acc[:, 1]
+        send(ct.at[it, other, pl.ds(yy * 4, 4)], cp.at[it, pl.ds(yy * 4, 4)], cp_s.at[it], cp_r.at[it, yy], cpart)
+
+    def pack(it, dy):
+        yy = (y + dy) % 4
+        arrived(cp.at[it, pl.ds(yy * 4, 4)], cp_r.at[it, yy])
+        for i in range(4):
+            mine, theirs = ct[it, core, yy * 4 + i], cp[it, yy * 4 + i]
+            pk[it, yy * 4 + i] = jnp.concatenate(
+                [jnp.where(own_first, mine, theirs), jnp.where(own_first, theirs, mine)], axis=1)
+
+    def to_mirror(it, dy, c):
+        rows = slice(c * 8, c * 8 + 8)
+        for dz in (2, 1, 3, 0):
+            if dy + dz:
+                jj = (y + dy) % 4 * 4 + (zhi + dz) % 4
+                send(pk.at[it, jj, rows], u.at[it, j, rows], u_s.at[it], u_r.at[it, c], dev(dy, dz))
+
+    def square(it):
+        u[it, j] = pk[it, j]
+        c = jnp.concatenate([ct[it, i % 2, i // 2] for i in range(32)], axis=0)
+        ch[...] = jnp.concatenate([c, jnp.zeros((768, 64), F32)], axis=1).T[:192] + drv[...]
+
+    def first_rhs():
+        return jnp.concatenate([jnp.concatenate([ball[0, k, q, :, h * 384:h * 384 + 384] for k in range(3)], axis=0)
+                                for h in (0, 1) for q in range(8)], axis=1)
+
+    def second_rhs():
+        return jnp.concatenate([bn[q, :, h * 384:h * 384 + 384] for h in (0, 1) for q in range(8)], axis=1)
+
+    def first_group(dy):
+        yy = (y + dy) % 4
+        arrived(rt.at[pl.ds(yy * 4, 4), :, pl.ds(pl.multiple_of(other * 3072, 3072), 3072)], c_r.at[yy])
+        product(0, dy, first_rhs)
+        pack(0, dy)
+        for c in range(3):
+            to_mirror(0, dy, c)
+
     for p in (0, 1):
         ahead(j, p, dev(0, 1))
         ahead(j, p, dev(0, 3))
@@ -200,82 +243,51 @@
         ahead(j, p, dev(3, 0))
     for d in (1, 3):
         ahead(j, 2, dev(d, 0))
-    spread_b(None)
     for p in (0, 1, 2):
         to_core(j, p)
     for p in (0, 1):
         for d in (3, 1):
             event(0, d, p)
             event(d, 0, p)
+    spread_b(None)
     ahead(j, 2, dev(2, 0))
+    event(1, 0, 2)
+    event(3, 0, 2)
+    for p in (0, 1):
+        event(0, 2, p)
+        event(2, 0, p)
+    event(2, 0, 2)
     for d in (1, 3, 2):
         ahead(j, 2, dev(0, d))
     onward_b(None, 0)
-    event(1, 0, 2)
-    event(3, 0, 2)
-    for p in (0, 1):
-        event(0, 2, p)
-        event(2, 0, p)
-    event(2, 0, 2)
+    for dz in (3, 1):
+        for dy in (3, 1):
+            event(dy, dz, 0)
     partner_b(None)
-    for p in (0, 1):
-        for dz in (3, 1):
-            for dy in (3, 1):
-                event(dy, dz, p)
-    onward_b(None, 1)
+    for dz in (3, 1):
+        for dy in (3, 1):
+            event(dy, dz, 1)
     for p in (0, 1):
         for dy in (3, 1):
             event(dy, 2, p)
+    onward_b(None, 1)
+    for dz in (1, 3, 2):
+        event(0, dz, 2)
+    last_b(None)
+    loads[2].wait()
+    for dy in (1, 3):
+        for dz in (1, 3, 2):
+            event(dy, dz, 2)
     for p in (0, 1):
         for dz in (3, 1):
             event(2, dz, p)
+    for p in (0, 1):
+        event(2, 2, p)
     for dz in (1, 3, 2):
-        for dy in (0, 1, 3, 2):
-            event(dy, dz, 2)
-    for p in (0, 1):
-        event(2, 2, p)
-    last_b(None)
-    arrived(rt.at[:, :, pl.ds(pl.multiple_of(other * 3072, 3072), 3072)], c_r)
-
-    def cycle(it, rhs):
-        steps = (2, 1, 3, 0)
-        slabs = [(y + d) % 4 for d in steps]
-
-        def product(yy):
-            left = rt[pl.ds(yy * 4, 4)].reshape(192, 6144)
-            acc = lax.dot_general(left, rhs(), NT, preferred_element_type=F32).reshape(4, 2, 24, 192)
-            ct[it, 0, pl.ds(yy * 4, 4)] = acc[:, 0]
-            ct[it, 1, pl.ds(yy * 4, 4)] = acc[:, 1]
-            send(ct.at[it, other, pl.ds(yy * 4, 4)], cp.at[it, pl.ds(yy * 4, 4)], cp_s.at[it], cp_r.at[it, yy], cpart)
-
-        def to_mirror(dy, c):
-            rows = slice(c * 8, c * 8 + 8)
-            for dz in (2, 1, 3, 0):
-                if dy + dz:
-                    jj = (y + dy) % 4 * 4 + (zhi + dz) % 4
-                    send(pk.at[it, jj, rows], u.at[it, j, rows], u_s.at[it], u_r.at[it, c], dev(dy, dz))
-
-        def pack(g):
-            yy = slabs[g]
-            arrived(cp.at[it, pl.ds(yy * 4, 4)], cp_r.at[it, yy])
-            for i in range(4):
-                mine, theirs = ct[it, core, yy * 4 + i], cp[it, yy * 4 + i]
-                pk[it, yy * 4 + i] = jnp.concatenate(
-                    [jnp.where(own_first, mine, theirs), jnp.where(own_first, theirs, mine)], axis=1)
-            to_mirror(steps[g], 0)
-
-        product(slabs[0])
-        for g in range(1, 4):
-            product(slabs[g])
-            pack(g - 1)
-        pack(3)
-        for c in (1, 2):
-            for dy in steps:
-                to_mirror(dy, c)
-        u[it, j] = pk[it, j]
-        square = jnp.concatenate([ct[it, i % 2, i // 2] for i in range(32)], axis=0)
-        square = jnp.concatenate([square, jnp.zeros((768, 64), F32)], axis=1).T[:192]
-        ch[...] = square + drv[...]
+        event(2, dz, 2)
+    for dy in (2, 1, 3, 0):
+        first_group(dy)
+    square(0)
 
     def mirror(it, c):
         rows = slice(c * 8, c * 8 + 8)
@@ -299,15 +311,6 @@
         ball[1, c, s] = update(0, c).reshape(64, 768).astype(BF16)
         spread_b(c)
 
-    def first_rhs():
-        return jnp.concatenate([jnp.concatenate([ball[0, k, q, :, h * 384:h * 384 + 384] for k in range(3)], axis=0)
-                                for h in (0, 1) for q in range(8)], axis=1)
-
-    def second_rhs():
-        return jnp.concatenate([bn[q, :, h * 384:h * 384 + 384] for h in (0, 1) for q in range(8)], axis=1)
-
-    loads[2].wait()
-    cycle(0, first_rhs)
     mirror(0, 0)
     mirror(0, 1)
     next_b(0)
@@ -328,7 +331,18 @@
     for q in range(8):
         thirds = [ball[1, k, q].astype(F32).reshape(8, 8, 768) for k in range(3)]
         bn[q] = jnp.concatenate([thirds[i % 3][i // 3] for i in range(24)], axis=0).astype(BF16)
-    cycle(1, second_rhs)
+    steps = (2, 1, 3, 0)
+    product(1, steps[0], second_rhs)
+    for g in range(1, 4):
+        product(1, steps[g], second_rhs)
+        pack(1, steps[g - 1])
+        to_mirror(1, steps[g - 1], 0)
+    pack(1, steps[3])
+    to_mirror(1, steps[3], 0)
+    for c in (1, 2):
+        for dy in steps:
+            to_mirror(1, dy, c)
+    square(1)
     for c in range(3):
         mirror(1, c)
     for c in range(3):
@@ -370,11 +384,11 @@
             pltpu.VMEM((2, 8, 24, 768), F32),
             pltpu.VMEM((2, 8, 24, 768), F32),
             pltpu.VMEM((192, 768), F32),
-            dma((3,)), dma, dma, dma, dma, dma, dma((16, 3)), dma, dma, dma((2,)), dma((8, 2)), dma((3, 8, 2)),
+            dma((3,)), dma, dma, dma, dma, dma, dma((16, 3)), dma, dma((4,)), dma((2,)), dma((8, 2)), dma((3, 8, 2)),
             dma((2,)), dma((2, 4)), dma((2,)), dma((2, 3)), dma((2,)), dma((2, 3)),
         ],
         compiler_params=pltpu.CompilerParams(
-            collective_id=0, has_side_effects=True, vmem_limit_bytes=48 * 2**20),
+            collective_id=0, has_side_effects=True, vmem_limit_bytes=63 * 2**20),
         cost_estimate=pl.CostEstimate(flops=2 * 2 * 192 * 768 * 6144, bytes_accessed=3 * 2**20, transcendentals=0),
     )(amplitudes, driving, rloc, vir_energy.reshape(1, -1), vir_irrep.reshape(1, -1),
       occ_energy.reshape(1, -1), occ_irrep.reshape(1, -1), slab)

time: 141 us -> 139 us (0.986)
  local copies, waits for them, and re-layouts: 5.28 us -> 3.83 us
    unnamed x15 -> x3, local copies, waits for them, and re-layouts: 4.56 us -> 1.92 us
where the time goes in v4:
time: 139 us; the launch traced here: 138 us
  Pallas kernels  134 us (96%)
  local copies, waits for them, and re-layouts  3.83 us (3%)
    pallas_call x1, Pallas kernels, local(): pl.pallas_call(kernel, out_shape=jax.ShapeDtypeStruct((8, 24, cols), F32)...  134 us

profile of v4, /device:TPU:1, one launch (start us, length us, event | category | flops | bytes accessed | tf_op | source)
XLA Modules:
  0.0 138.3 jit_solution(15478509763750482322)
XLA Ops:
  0.0 0.0 copy-start
  0.0 1.3 reshape.20.viri
  1.3 0.0 copy-done
  1.3 0.6 reshape.19.vire
  1.9 134.5 %shard_map.82 = f32[8,24,768]{2,1,0:T(8,128)} custom-call(f32[192,768]{1,0:T(8,128)} %amp_h.1, f32[192,768]{1,0:T(8,128)} %drv_h.1, bf16[8,24,768]{2,1,0:T(8,128)(2,1)} %bitcast.7, f32[1,1536]{1,0:T(1,128)} %reshape.19.vire, s32[1,1536]{1,0:T(1,128)} %reshape.20.viri, f32[1,128]{1,0:T(1,128)} %bitcast.8, s32[1,128]{1,0:T(1,128)} %bitcast.9, s32[4]{0:T(128)} %slab.1), custom_call_target="tpu_custom_call" | custom-call | flops 3623878656 | bytes 3145728 | tf_op jit(solution)/shard_map/pallas_call | solution.py:366
  136.4 1.9 %copy.10 = f32[192,768]{1,0:T(8,128)} copy(f32[192,768]{1,0:T(8,128)} %bitcast.6) | data formatting | bytes 1179648
Async XLA Ops:
  0.0 1.3 copy-start

commit v5 on v4

--- a/solution.py
+++ b/solution.py
@@ -94,12 +94,14 @@
         return part
 
     picked = [slab_at(i) for i in range(4)]
-    vce, vci = tile_part(vire[...]), tile_part(viri[...])
+    vir_e = jnp.concatenate([vire[i:i + 1] for i in range(12)], axis=1)
+    vir_i = jnp.concatenate([viri[i:i + 1] for i in range(12)], axis=1)
+    vce, vci = tile_part(vir_e), tile_part(vir_i)
     cole = jnp.concatenate([vce - picked[i][0] for i in range(4)], axis=1)
     coli = jnp.concatenate([jnp.bitwise_xor(vci, picked[i][1]) for i in range(4)], axis=1)
     rowe_v, rowi_v = slab_at(y)
-    rowe_l = row_part(vire[...]) - rowe_v
-    rowi_l = jnp.bitwise_xor(row_part(viri[...]), rowi_v).astype(F32)
+    rowe_l = row_part(vir_e) - rowe_v
+    rowi_l = jnp.bitwise_xor(row_part(vir_i), rowi_v).astype(F32)
 
     def stand(line):
         wide = jnp.concatenate([line, jnp.zeros((1, 64), F32)], axis=1)
@@ -390,7 +392,7 @@
         compiler_params=pltpu.CompilerParams(
             collective_id=0, has_side_effects=True, vmem_limit_bytes=63 * 2**20),
         cost_estimate=pl.CostEstimate(flops=2 * 2 * 192 * 768 * 6144, bytes_accessed=3 * 2**20, transcendentals=0),
-    )(amplitudes, driving, rloc, vir_energy.reshape(1, -1), vir_irrep.reshape(1, -1),
+    )(amplitudes, driving, rloc, vir_energy.reshape(12, 128), vir_irrep.reshape(12, 128),
       occ_energy.reshape(1, -1), occ_irrep.reshape(1, -1), slab)
     return result.reshape(rows, cols)
 

time: 139 us -> 136 us (0.978)
  local copies, waits for them, and re-layouts: 3.83 us -> 1.92 us
    reshape x2 -> x0, local copies, waits for them, and re-layouts: 1.91 us -> none  [the longest x1 1.31 us: local(): vir_irrep.reshape(1, -1)]
where the time goes in v5:
time: 136 us
  Pallas kernels  134 us (99%)
  local copies, waits for them, and re-layouts  1.92 us (1%)
    pallas_call x1, Pallas kernels, local(): pl.pallas_call(kernel, out_shape=jax.ShapeDtypeStruct((8, 24, cols), F32)...  134 us

profile of v5, /device:TPU:1, one launch (start us, length us, event | category | flops | bytes accessed | tf_op | source)
XLA Modules:
  0.0 136.0 jit_solution(11016555716615562740)
XLA Ops:
  0.0 134.1 %shard_map.82 = f32[8,24,768]{2,1,0:T(8,128)} custom-call(f32[192,768]{1,0:T(8,128)} %amp_h.1, f32[192,768]{1,0:T(8,128)} %drv_h.1, bf16[8,24,768]{2,1,0:T(8,128)(2,1)} %bitcast.9, f32[12,128]{1,0:T(8,128)} %bitcast.10, s32[12,128]{1,0:T(8,128)} %bitcast.11, f32[1,128]{1,0:T(1,128)} %bitcast.12, s32[1,128]{1,0:T(1,128)} %bitcast.13, s32[4]{0:T(128)} %slab.1), custom_call_target="tpu_custom_call" | custom-call | flops 3623878656 | bytes 3145728 | tf_op jit(solution)/shard_map/pallas_call | solution.py:368
  134.1 1.9 %copy.10 = f32[192,768]{1,0:T(8,128)} copy(f32[192,768]{1,0:T(8,128)} %bitcast.8) | data formatting | bytes 1179648

commit v6 on v5

--- a/solution.py
+++ b/solution.py
@@ -59,19 +59,20 @@
         ball[0, k, s] = amp[k * 64:k * 64 + 64].astype(BF16)
     arrived(rpair, p_r)
     own_first = core == 0
-    for q in range(8):
+    def kslot(q):
+        return pl.ds(pl.multiple_of(core * 3072 + q * 384, 384), 384)
+
+    def both_cores(q):
         a = rloc[q].astype(F32)
         b = rpair[q].astype(F32)
         both = jnp.concatenate([jnp.where(own_first, a, b), jnp.where(own_first, b, a)], axis=0).astype(BF16)
-        rsend[q] = jnp.where(own_first, both[:, :384], both[:, 384:])
-
-    def kslot(q):
-        return pl.ds(pl.multiple_of(core * 3072 + q * 384, 384), 384)
-
-    for d in range(1, 8):
+        return jnp.where(own_first, both[:, :384], both[:, 384:])
+
+    for d in (2, 6, 1, 3, 5, 7, 4):
         q = (s + d) % 8
+        rsend[q] = both_cores(q)
         send(rsend.at[q], rt.at[j, :, kslot(s)], a_s, a_r, (q, t))
-    rt[j, :, kslot(s)] = rsend[s]
+    rt[j, :, kslot(s)] = both_cores(s)
 
     hot = lax.broadcasted_iota(jnp.int32, (1, 128), 1)
 
@@ -347,8 +348,9 @@
     square(1)
     for c in range(3):
         mirror(1, c)
-    for c in range(3):
-        out[:, c * 8:c * 8 + 8] = update(1, c)
+        if c:
+            out[:, c * 8 - 8:c * 8] = update(1, c - 1)
+    out[:, 16:24] = update(1, 2)
     sent(rloc, p_s)
     sent(rsend.at[0:7], a_s)
     sent(rt.at[0:15, :, 0:3072], g_s)

time: 136 us -> 137 us (level); the launches traced: 136 us -> 136 us
  no operation moved by 1% of the time
where the time goes in v6:
time: 137 us; the launch traced here: 136 us
  Pallas kernels  134 us (98%)
  local copies, waits for them, and re-layouts  1.92 us (1%)
    pallas_call x1, Pallas kernels, local(): pl.pallas_call(kernel, out_shape=jax.ShapeDtypeStruct((8, 24, cols), F32)...  134 us

profile of v6, /device:TPU:1, one launch (start us, length us, event | category | flops | bytes accessed | tf_op | source)
XLA Modules:
  0.0 135.6 jit_solution(891002520318333082)
XLA Ops:
  0.0 133.7 %shard_map.82 = f32[8,24,768]{2,1,0:T(8,128)} custom-call(f32[192,768]{1,0:T(8,128)} %amp_h.1, f32[192,768]{1,0:T(8,128)} %drv_h.1, bf16[8,24,768]{2,1,0:T(8,128)(2,1)} %bitcast.9, f32[12,128]{1,0:T(8,128)} %bitcast.10, s32[12,128]{1,0:T(8,128)} %bitcast.11, f32[1,128]{1,0:T(1,128)} %bitcast.12, s32[1,128]{1,0:T(1,128)} %bitcast.13, s32[4]{0:T(128)} %slab.1), custom_call_target="tpu_custom_call" | custom-call | flops 3623878656 | bytes 3145728 | tf_op jit(solution)/shard_map/pallas_call | solution.py:370
  133.7 1.9 %copy.10 = f32[192,768]{1,0:T(8,128)} copy(f32[192,768]{1,0:T(8,128)} %bitcast.8) | data formatting | bytes 1179648

commit v7 on v5

--- a/solution.py
+++ b/solution.py
@@ -10,7 +10,7 @@
 F32, BF16 = jnp.float32, jnp.bfloat16
 
 
-PIECES = ((0, 1408), (1408, 1280), (2688, 384))
+PIECES = ((0, 1408), (1408, 1408), (2816, 256))
 
 
 def kernel(amp_h, drv_h, rloc_h, vire, viri, occe, occi, slab, out,

time: 136 us -> 137 us (level)
  no operation moved by 1% of the time
where the time goes in v7:
time: 137 us; the launch traced here: 136 us
  Pallas kernels  134 us (98%)
  local copies, waits for them, and re-layouts  1.92 us (1%)
    pallas_call x1, Pallas kernels, local(): pl.pallas_call(kernel, out_shape=jax.ShapeDtypeStruct((8, 24, cols), F32)...  134 us

profile of v7, /device:TPU:1, one launch (start us, length us, event | category | flops | bytes accessed | tf_op | source)
XLA Modules:
  0.0 136.3 jit_solution(3611903685339631573)
XLA Ops:
  0.0 134.4 %shard_map.82 = f32[8,24,768]{2,1,0:T(8,128)} custom-call(f32[192,768]{1,0:T(8,128)} %amp_h.1, f32[192,768]{1,0:T(8,128)} %drv_h.1, bf16[8,24,768]{2,1,0:T(8,128)(2,1)} %bitcast.9, f32[12,128]{1,0:T(8,128)} %bitcast.10, s32[12,128]{1,0:T(8,128)} %bitcast.11, f32[1,128]{1,0:T(1,128)} %bitcast.12, s32[1,128]{1,0:T(1,128)} %bitcast.13, s32[4]{0:T(128)} %slab.1), custom_call_target="tpu_custom_call" | custom-call | flops 3623878656 | bytes 3145728 | tf_op jit(solution)/shard_map/pallas_call | solution.py:368
  134.4 1.9 %copy.10 = f32[192,768]{1,0:T(8,128)} copy(f32[192,768]{1,0:T(8,128)} %bitcast.8) | data formatting | bytes 1179648
